TPU v7x, 128 devices: a whole 4x4x4 slice. The times are simulated.
128 devices in a mesh: seq: 8 (over x, core), head: 16 (over z, y).
Axes of the slice: x: 4, y: 4, z: 4, core: 2. Of those that a mesh axis runs over, the one named last changes fastest.
Arguments:
- tokens: bfloat16 [1024, 6144], P('seq'), may hold values from -6 to 6
- log_decay: float32 [1024, 32], P('seq', 'head'), may hold values from -1 to 0
- carried_state: float32 [32, 128, 128], P('head'), may hold values from -48 to 48
- q_weight: bfloat16 [6144, 4096], P(None, 'head'), may hold values from -0.078125 to 0.078125
- k_weight: bfloat16 [6144, 4096], P(None, 'head'), may hold values from -0.078125 to 0.078125
- v_weight: bfloat16 [6144, 4096], P(None, 'head'), may hold values from -0.078125 to 0.078125
- out_weight: bfloat16 [4096, 6144], P('head'), may hold values from -0.09375 to 0.09375
- final_gain: bfloat16 [6144], replicated, may hold values from 0.099609375 to 1.8984375
- vocab_weight: bfloat16 [6144, 131072], P(None, ('seq', 'head')), may hold values from -5 to 5
- targets: int32 [1024], replicated, may hold values from 0 to 131071
Outputs:
- loglik: float32 [1024], P('seq')
All inputs are finite; a program needn't handle non-finite values.
Results may differ from a plain program's by a relative error of at most 0.002.
Values may be sent and summed in bfloat16 or wider, within the bound.
No kernel may reach another device: no remote copies, remote signals or barrier semaphores. Data moves between devices by JAX's collectives and lax.ppermute only.
A program may use at most 128 MiB of HBM per device.

v0:
```python
import jax
import jax.numpy as jnp
from jax import lax
from jax.sharding import PartitionSpec as P


def prefix(array, axis, combine, identity):
    length, here = (lax.axis_size(axis), lax.axis_index(axis))
    everything = jax.tree.map(lambda part: lax.all_gather(part, axis), array)
    start = jax.tree.map(
        lambda part, zero: jnp.broadcast_to(jnp.asarray(zero, part.dtype), part.shape),
        array,
        identity,
    )

    def turn(k, before):
        reached = k < here
        new = combine(before, jax.tree.map(lambda part: part[k], everything))
        return jax.tree.map(lambda a, b: jnp.where(reached, a, b), new, before)

    return lax.fori_loop(0, length, turn, start)


def combine_states(earlier, later):
    return (earlier[0] * later[0], later[0][:, None, None] * earlier[1] + later[1])


def shards(
    tokens,
    log_decay,
    carried_state,
    q_weight,
    k_weight,
    v_weight,
    out_weight,
    final_gain,
    vocab_weight,
    targets,
):
    highest = lax.Precision.HIGHEST
    rows_here = tokens.shape[0]
    heads_here = carried_state.shape[0]
    head_size = carried_state.shape[1]
    view = (rows_here, heads_here, head_size)
    queries = (
        jnp.dot(tokens, q_weight, preferred_element_type=jnp.float32)
        .astype(jnp.bfloat16)
        .reshape(view)
    )
    keys_loc = (
        jnp.dot(tokens, k_weight, preferred_element_type=jnp.float32)
        .astype(jnp.bfloat16)
        .reshape(view)
    )
    values = (
        jnp.dot(tokens, v_weight, preferred_element_type=jnp.float32)
        .astype(jnp.bfloat16)
        .reshape(view)
    )
    cumul = jnp.cumsum(log_decay, axis=0)
    last_cum = cumul[-1]
    ends = jnp.exp(last_cum[None, :] - cumul)
    local_state = jnp.einsum(
        "thd,the->hde",
        keys_loc.astype(jnp.float32) * ends[:, :, None],
        values.astype(jnp.float32),
        precision=highest,
    )
    total_decay = jnp.exp(last_cum)
    prefix_decay, prefix_state = prefix(
        (total_decay, local_state),
        "seq",
        combine_states,
        (jnp.ones_like(total_decay), jnp.zeros_like(local_state)),
    )
    lower = jnp.arange(rows_here)[:, None] >= jnp.arange(rows_here)[None, :]
    scores = jnp.einsum("thd,shd->hts", queries, keys_loc, preferred_element_type=jnp.float32)
    diff = jnp.transpose(cumul[:, None, :] - cumul[None, :, :], (2, 0, 1))
    weight = (scores * jnp.exp(jnp.where(lower[None], diff, -1e30))).astype(jnp.bfloat16)
    intra = jnp.einsum("hts,shd->thd", weight, values, preferred_element_type=jnp.float32)
    state_in = prefix_decay[:, None, None] * carried_state + prefix_state
    inter = jnp.exp(cumul)[:, :, None] * jnp.einsum(
        "thd,hde->the", queries.astype(jnp.float32), state_in, precision=highest
    )
    attended = intra + inter
    normed_heads = attended * lax.rsqrt(
        jnp.mean(attended * attended, axis=-1, keepdims=True) + 1e-06
    )
    flat_heads = normed_heads.astype(jnp.bfloat16).reshape(rows_here, heads_here * head_size)
    rows_mine = rows_here // lax.axis_size("head")
    head_index = lax.axis_index("head")
    mixed_all = lax.psum(
        jnp.dot(flat_heads, out_weight, preferred_element_type=jnp.float32), "head"
    )
    mixed = lax.dynamic_slice_in_dim(mixed_all, head_index * rows_mine, rows_mine, 0)
    resid = (
        lax.dynamic_slice_in_dim(tokens, head_index * rows_mine, rows_mine, 0).astype(jnp.float32)
        + mixed
    )
    final_rows = (
        resid
        * lax.rsqrt(jnp.mean(resid * resid, axis=-1, keepdims=True) + 1e-06)
        * final_gain.astype(jnp.float32)
    )
    final_rows = final_rows.astype(jnp.bfloat16)
    vocab_local = vocab_weight.shape[1]
    offset = (lax.axis_index("seq") * lax.axis_size("head") + head_index) * vocab_local
    columns = jnp.arange(vocab_local, dtype=jnp.int32)
    logits = jnp.dot(
        lax.all_gather(final_rows, ("seq", "head"), axis=0, tiled=True),
        vocab_weight,
        preferred_element_type=jnp.float32,
    )
    top = jnp.max(logits, axis=1)
    total = jnp.sum(jnp.exp(logits - top[:, None]), axis=1)
    wanted = targets - offset
    hit = jnp.sum(jnp.where(columns[None, :] == wanted[:, None], logits, 0.0), axis=1)
    top_all = lax.pmax(top, ("seq", "head"))
    total_all, hit_all = lax.psum((total * jnp.exp(top - top_all), hit), ("seq", "head"))
    loglik = hit_all - top_all - jnp.log(total_all)
    return lax.dynamic_slice_in_dim(loglik, lax.axis_index("seq") * rows_here, rows_here, 0)


def solution(mesh):
    return jax.shard_map(
        shards,
        mesh=mesh,
        in_specs=(
            P("seq", None),
            P("seq", "head"),
            P("head", None, None),
            P(None, "head"),
            P(None, "head"),
            P(None, "head"),
            P("head", None),
            P(),
            P(None, ("seq", "head")),
            P(),
        ),
        out_specs=P("seq"),
        check_vma=False,
    )
```

profile of v0, /device:TPU:1, one launch (start us, length us, event | category | flops | bytes accessed | tf_op | source)
XLA Modules:
  0.0 385.3 jit_solution(14718534888018662489)
XLA Ops:
  6.5 0.0 copy-start
  6.5 0.0 all-gather.7.cloned.1.call-start
  6.5 0.9 copy.23
  7.5 0.2 reduce_window_sum.11
  7.7 0.1 copy.30
  7.7 3.0 convolution_convert_fusion
  10.7 0.1 copy.36
  10.8 3.0 fusion.4
  13.8 0.9 fusion.8
  14.6 0.0 all-gather.7.cloned.1.call-update
  14.7 0.0 all-reduce.3.cloned.1.call-start
  14.7 11.8 %all-gather.1 = f32[8,1,2]{2,1,0:T(1,128)S(1)} all-gather(f32[1,1,2]{2,1,0:T(1,128)S(1)} %get-tuple-element.171), channel_id=1, replica_groups=mesh['seq'=8,'head'=16] {'seq'}, dimensions={0}, use_global_device_ids=true | all-gather | bytes 72 | tf_op jit(solution)/shard_map/all_gather | solution.py:9
  26.5 0.1 copy.27
  26.6 0.1 copy.24
  26.7 3.1 fusion.5
  29.8 12.0 %all-gather.7.cloned.1.call-done = f32[16,128,128]{2,1,0:T(8,128)} async-done(((f32[2,128,128]{2,1,0:T(8,128)}), f32[16,128,128]{2,1,0:T(8,128)}) %all-gather.7.cloned.1.call-update) | async-done | bytes 1048592 | tf_op jit(solution)/shard_map/all_gather | solution.py:9
  41.8 8.3 %while.16 = (s32[]{:T(128)}, f32[2]{0:T(128)S(1)}, f32[2,128,128]{2,1,0:T(8,128)S(1)}, s32[]{:T(128)}, f32[8,2]{1,0:T(8,128)S(1)}, /*index=5*/f32[8,2,128,128]{3,2,1,0:T(8,128)}, s32[]{:T(128)}, s32[]{:T(128)}) while((s32[]{:T(128)}, f32[2]{0:T(128)S(1)}, f32[2,128,128]{2,1,0:T(8,128)S(1)}, s32[]{:T(128)}, f32[8,2]{1,0:T(8,128)S(1)}, ...), condition=%wide.region_2.3_spmd.clone, body=%wide.region_1.2_spmd.clone.sunk | while | flops 131082 | bytes 393371 | solution.py:21
  41.8 1.0 fusion.48
  42.8 1.0 fusion.48
  43.9 1.0 fusion.48
  44.9 1.0 fusion.48
  46.0 1.0 fusion.48
  47.0 1.0 fusion.48
  48.0 1.0 fusion.48
  49.1 1.0 fusion.48
  50.1 1.9 fusion.1
  52.0 1.2 multiply_reduce_fusion.1
  53.3 0.0 copy-done
  53.3 2.3 fusion.35
  55.6 0.0 copy-start.1
  55.6 0.0 copy-start.2
  55.6 0.0 all-reduce.3.cloned.1.call-update
  55.6 0.0 all-gather.5.cloned.1.call-start
  55.7 0.6 copy-done.1
  56.3 94.3 %all-reduce.3.cloned.1.call-done = f32[128,6144]{1,0:T(8,128)} async-done(((f32[128,6144]{1,0:T(8,128)}), f32[128,6144]{1,0:T(8,128)}) %all-reduce.3.cloned.1.call-update) | async-done | bytes 3145744 | tf_op jit(solution)/shard_map/psum | solution.py:92
  150.6 1.2 multiply_reduce_fusion
  151.8 1.7 multiply_convert_fusion
  153.5 0.0 all-gather.5.cloned.1.call-update
  153.5 0.0 copy-done.2
  153.6 73.3 %all-gather.5.cloned.1.call-done = bf16[1024,6144]{1,0:T(8,128)(2,1)} async-done(((bf16[8,6144]{1,0:T(8,128)(2,1)}), bf16[1024,6144]{1,0:T(8,128)(2,1)}) %all-gather.5.cloned.1.call-update) | async-done | bytes 12582928 | tf_op jit(solution)/shard_map/all_gather | solution.py:110
  226.9 19.4 %fusion.34 = (f32[1024]{0:T(1024)S(1)}, f32[1024,1024]{0,1:T(8,128)}) fusion(bf16[1024,6144]{1,0:T(8,128)(2,1)} %all-gather.5.cloned.1.call-done, bf16[6144,1024]{1,0:T(8,128)(2,1)} %param.20), kind=kOutput, calls=%fused_computation.57 | convolution fusion | flops 12885949440 | bytes 29364224 | tf_op jit(solution)/shard_map/dot_general | solution.py:109
  246.3 64.4 %pmax.7 = f32[1024]{0:T(1024)S(1)} all-reduce(f32[1024]{0:T(1024)S(1)} %get-tuple-element.174), channel_id=1, replica_groups=mesh['seq'=8,'head'=16] {'seq','head'}, use_global_device_ids=true, to_apply=%region_9.10 | all-reduce | flops 1024 | bytes 8192 | tf_op jit(solution)/shard_map/pmax | solution.py:118
  310.7 3.3 select_reduce_fusion
  314.0 64.2 %all-reduce = (f32[1024]{0:T(1024)S(1)}, f32[1024]{0:T(1024)S(1)}) all-reduce(f32[1024]{0:T(1024)S(1)} %exponential_multiply_fusion, f32[1024]{0:T(1024)S(1)} %get-tuple-element.150), channel_id=1, replica_groups=mesh['seq'=8,'head'=16] {'seq','head'}, use_global_device_ids=true, to_apply=%region_11.12 | all-reduce | flops 2048 | bytes 16384 | tf_op jit(solution)/shard_map/psum | solution.py:119
  378.2 0.6 dynamic_slice.25
  (20 shorter events, 0.3 us)
Async XLA Ops:
  6.5 46.7 %copy-start = (bf16[256,6144]{1,0:T(8,128)(2,1)S(1)}, bf16[256,6144]{1,0:T(8,128)(2,1)}, u32[]{:S(2)}) copy-start(bf16[256,6144]{1,0:T(8,128)(2,1)} %param.18) | copy-start | bytes 9437188
  6.5 35.2 %all-gather.7.cloned.1.call-start = ((), (), s32[]{:S(2)}) async-start(), calls=%async_computation.2 | async-start | bytes 1179648 | tf_op jit(solution)/shard_map/all_gather | solution.py:9
  14.7 135.9 %all-reduce.3.cloned.1.call-start = ((), (), s32[]{:S(2)}) async-start(), calls=%async_computation | async-start | bytes 6291456 | tf_op jit(solution)/shard_map/psum | solution.py:92
  55.6 0.7 copy-start.1
  55.6 98.0 %copy-start.2 = (s32[1024]{0:T(1024)S(1)}, s32[1024]{0:T(1024)}, u32[]{:S(2)}) copy-start(s32[1024]{0:T(1024)} %param.21) | copy-start | bytes 12292
  55.6 171.3 %all-gather.5.cloned.1.call-start = ((), (), s32[]{:S(2)}) async-start(), calls=%async_computation.1 | async-start | bytes 12681216 | tf_op jit(solution)/shard_map/all_gather | solution.py:110
Sparse Core Ops, SparseCore 0:
  14.8 26.9 all-gather.6
  55.7 94.8 all-reduce.2
  153.7 73.0 all-gather.4
where the time goes:
time: 386 us; the launch traced here: 385 us
  waiting for transfers between devices  180 us (47%)
  blocking collectives  140 us (36%)
  matrix products  34.7 us (9%)
  other arithmetic  14.5 us (4%)
  between operations  13.2 us (3%)
    psum x1, waiting for transfers between devices, shards(): lax.psum(jnp.dot(flat_heads, out_weight, preferred_element_type=jnp.float...  94.3 us
    all_gather x1, waiting for transfers between devices, shards(): lax.all_gather(final_rows, ('seq', 'head'), axis=0, tiled=True)  73.3 us
    pmax x1, blocking collectives, shards(): top_all = lax.pmax(top, ('seq', 'head'))  64.4 us
    psum x1, blocking collectives, shards(): lax.psum((total * jnp.exp(top - top_all), hit), ('seq', 'head'))  64.2 us
    dot_general x1, matrix products, shards(): jnp.dot(lax.all_gather(final_rows, ('seq', 'head'), axis=0, tiled=True),...  19.4 us
    all_gather x1, waiting for transfers between devices, prefix(): everything = jax.tree.map(lambda part: lax.all_gather(part, axis), array)  12 us
    all_gather x1, blocking collectives, prefix(): everything = jax.tree.map(lambda part: lax.all_gather(part, axis), array)  11.8 us
    select_n x16, other arithmetic, turn(): return jax.tree.map(lambda a, b: jnp.where(reached, a, b), new, before)  8.09 us
  transfers between devices with their start and end apart: 3, of which 3 were waited for; matrix products, arithmetic and copies ran while one was open for 1% of the time, Pallas kernels for 0%

commit v1 on v0

--- a/solution.py
+++ b/solution.py
@@ -107,7 +107,12 @@
     offset = (lax.axis_index("seq") * lax.axis_size("head") + head_index) * vocab_local
     columns = jnp.arange(vocab_local, dtype=jnp.int32)
     logits = jnp.dot(
-        lax.all_gather(final_rows, ("seq", "head"), axis=0, tiled=True),
+        jnp.concatenate(
+            lax.all_to_all(
+                jnp.stack([final_rows] * lax.axis_size(("seq", "head"))), ("seq", "head"), 0, 0
+            ),
+            axis=0,
+        ),
         vocab_weight,
         preferred_element_type=jnp.float32,
     )

time: 386 us -> 483 us (1.25)
  waiting for transfers between devices: 180 us -> 261 us
  starting transfers between devices: 0.09 us -> 8.1 us
  local copies, waits for them, and re-layouts: 2.47 us -> 8.56 us
    all_to_all x0 -> x1, waiting for transfers between devices: none -> 154 us  [shards(): lax.all_to_all(jnp.stack([final_rows] * lax.axis_size(('seq', 'head'))),...]
    all_gather x1 -> x0, waiting for transfers between devices: 73.3 us -> none  [shards(): lax.all_gather(final_rows, ('seq', 'head'), axis=0, tiled=True)]
    all_to_all x0 -> x1, starting transfers between devices: none -> 8.06 us  [shards(): lax.all_to_all(jnp.stack([final_rows] * lax.axis_size(('seq', 'head'))),...]
    another operation x0 -> x1, local copies, waits for them, and re-layouts: none -> 6.04 us  [shards(): jnp.stack([final_rows] * lax.axis_size(('seq', 'head')))]
where the time goes in v1:
time: 483 us; the launch traced here: 482 us
  waiting for transfers between devices  261 us (54%)
  blocking collectives  143 us (30%)
  matrix products  34.7 us (7%)
  other arithmetic  13.9 us (3%)
  between operations  13.5 us (3%)
  local copies, waits for them, and re-layouts  8.56 us (2%)
  starting transfers between devices  8.1 us (2%)
    all_to_all x1, waiting for transfers between devices, shards(): lax.all_to_all(jnp.stack([final_rows] * lax.axis_size(('seq', 'head'))),...  154 us
    psum x1, waiting for transfers between devices, shards(): lax.psum(jnp.dot(flat_heads, out_weight, preferred_element_type=jnp.float...  94.3 us
    pmax x1, blocking collectives, shards(): top_all = lax.pmax(top, ('seq', 'head'))  66.8 us
    psum x1, blocking collectives, shards(): lax.psum((total * jnp.exp(top - top_all), hit), ('seq', 'head'))  64.2 us
    dot_general x1, matrix products, shards(): jnp.dot(jnp.concatenate(lax.all_to_all(jnp.stack([final_rows] * lax.axis_...  19.4 us
    all_gather x1, waiting for transfers between devices, prefix(): everything = jax.tree.map(lambda part: lax.all_gather(part, axis), array)  12 us
    all_gather x1, blocking collectives, prefix(): everything = jax.tree.map(lambda part: lax.all_gather(part, axis), array)  11.8 us
  transfers between devices with their start and end apart: 3, of which 3 were waited for; matrix products, arithmetic and copies ran while one was open for 1% of the time, Pallas kernels for 0%

profile of v1, /device:TPU:1, one launch (start us, length us, event | category | flops | bytes accessed | tf_op | source)
XLA Modules:
  0.0 482.5 jit_solution(2064878768983144396)
XLA Ops:
  6.5 0.0 copy-start
  6.5 0.0 all-gather.4.cloned.1.call-start
  6.5 0.9 copy.23
  7.5 0.2 reduce_window_sum.11
  7.7 0.1 copy.30
  7.7 3.0 convolution_convert_fusion
  10.7 0.1 copy.36
  10.8 3.0 fusion.6
  13.8 0.9 fusion.10
  14.6 0.0 all-gather.4.cloned.1.call-update
  14.7 0.0 all-reduce.3.cloned.1.call-start
  14.7 11.8 %all-gather.1 = f32[8,1,2]{2,1,0:T(1,128)S(1)} all-gather(f32[1,1,2]{2,1,0:T(1,128)S(1)} %get-tuple-element.171), channel_id=1, replica_groups=mesh['seq'=8,'head'=16] {'seq'}, dimensions={0}, use_global_device_ids=true | all-gather | bytes 72 | tf_op jit(solution)/shard_map/all_gather | solution.py:9
  26.5 0.1 copy.27
  26.6 0.1 copy.24
  26.7 3.1 fusion.7
  29.8 12.0 %all-gather.4.cloned.1.call-done = f32[16,128,128]{2,1,0:T(8,128)} async-done(((f32[2,128,128]{2,1,0:T(8,128)}), f32[16,128,128]{2,1,0:T(8,128)}) %all-gather.4.cloned.1.call-update) | async-done | bytes 1048592 | tf_op jit(solution)/shard_map/all_gather | solution.py:9
  41.8 8.3 %while.16 = (s32[]{:T(128)}, f32[2]{0:T(128)S(1)}, f32[2,128,128]{2,1,0:T(8,128)S(1)}, s32[]{:T(128)}, f32[8,2]{1,0:T(8,128)S(1)}, /*index=5*/f32[8,2,128,128]{3,2,1,0:T(8,128)}, s32[]{:T(128)}, s32[]{:T(128)}) while((s32[]{:T(128)}, f32[2]{0:T(128)S(1)}, f32[2,128,128]{2,1,0:T(8,128)S(1)}, s32[]{:T(128)}, f32[8,2]{1,0:T(8,128)S(1)}, ...), condition=%wide.region_2.3_spmd.clone, body=%wide.region_1.2_spmd.clone.sunk | while | flops 131082 | bytes 393371 | solution.py:21
  41.8 1.0 fusion.49
  42.8 1.0 fusion.49
  43.9 1.0 fusion.49
  44.9 1.0 fusion.49
  45.9 1.0 fusion.49
  47.0 1.0 fusion.49
  48.0 1.0 fusion.49
  49.1 1.0 fusion.49
  50.1 1.9 fusion.3
  52.0 1.2 multiply_reduce_fusion.1
  53.3 0.0 copy-done
  53.3 2.3 fusion.37
  55.6 0.0 copy-start.1
  55.6 0.0 all-reduce.3.cloned.1.call-update
  55.6 0.7 copy-done.1
  56.3 94.3 %all-reduce.3.cloned.1.call-done = f32[128,6144]{1,0:T(8,128)} async-done(((f32[128,6144]{1,0:T(8,128)}), f32[128,6144]{1,0:T(8,128)}) %all-reduce.3.cloned.1.call-update) | async-done | bytes 3145744 | tf_op jit(solution)/shard_map/psum | solution.py:92
  150.6 1.2 multiply_reduce_fusion
  151.8 1.1 multiply_convert_fusion
  152.9 6.0 %stack.2 = bf16[128,8,6144]{2,1,0:T(8,128)(2,1)} broadcast(bf16[8,6144]{1,0:T(8,128)(2,1)S(1)} %multiply_convert_fusion), dimensions={1,2} | broadcast | bytes 12681216 | tf_op jit(solution)/shard_map/stack | solution.py:112
  158.9 0.0 copy-start.2
  158.9 8.1 %all-to-all-start = ((bf16[128,8,6144]{2,1,0:T(8,128)(2,1)}), bf16[128,8,6144]{2,1,0:T(8,128)(2,1)}, u32[]{:S(2)}, u32[]{:S(2)}) async-start(bf16[128,8,6144]{2,1,0:T(8,128)(2,1)} %stack.2), calls=%async_computation | async-start | bytes 25165824 | tf_op jit(solution)/shard_map/all_to_all | solution.py:111
  167.0 0.0 copy-done.2
  167.0 154.3 %all-to-all-done = bf16[128,8,6144]{2,1,0:T(8,128)(2,1)} async-done(((bf16[128,8,6144]{2,1,0:T(8,128)(2,1)}), bf16[128,8,6144]{2,1,0:T(8,128)(2,1)}, u32[]{:S(2)}, u32[]{:S(2)}) %all-to-all-start) | async-done | bytes 12582944 | tf_op jit(solution)/shard_map/all_to_all | solution.py:111
  321.3 19.4 %fusion.36 = (f32[1024]{0:T(1024)S(1)}, f32[1024,1024]{0,1:T(8,128)}) fusion(bf16[6144,1024]{1,0:T(8,128)(2,1)} %param.20, bf16[128,8,6144]{2,1,0:T(8,128)(2,1)} %all-to-all-done), kind=kOutput, calls=%fused_computation.59 | convolution fusion | flops 12885949440 | bytes 29364224 | tf_op jit(solution)/shard_map/dot_general | solution.py:109
  340.7 66.8 %pmax.7 = f32[1024]{0:T(1024)S(1)} all-reduce(f32[1024]{0:T(1024)S(1)} %get-tuple-element.174), channel_id=1, replica_groups=mesh['seq'=8,'head'=16] {'seq','head'}, use_global_device_ids=true, to_apply=%region_9.10 | all-reduce | flops 1024 | bytes 8192 | tf_op jit(solution)/shard_map/pmax | solution.py:123
  407.5 3.3 select_reduce_fusion
  410.8 64.2 %all-reduce = (f32[1024]{0:T(1024)S(1)}, f32[1024]{0:T(1024)S(1)}) all-reduce(f32[1024]{0:T(1024)S(1)} %exponential_multiply_fusion, f32[1024]{0:T(1024)S(1)} %get-tuple-element.150), channel_id=1, replica_groups=mesh['seq'=8,'head'=16] {'seq','head'}, use_global_device_ids=true, to_apply=%region_11.12 | all-reduce | flops 2048 | bytes 16384 | tf_op jit(solution)/shard_map/psum | solution.py:124
  475.1 0.6 dynamic_slice.25
  (20 shorter events, 0.3 us)
Async XLA Ops:
  6.5 46.7 %copy-start = (bf16[256,6144]{1,0:T(8,128)(2,1)S(1)}, bf16[256,6144]{1,0:T(8,128)(2,1)}, u32[]{:S(2)}) copy-start(bf16[256,6144]{1,0:T(8,128)(2,1)} %param.18) | copy-start | bytes 9437188
  6.5 35.2 %all-gather.4.cloned.1.call-start = ((), (), s32[]{:S(2)}) async-start(), calls=%async_computation.2 | async-start | bytes 1179648 | tf_op jit(solution)/shard_map/all_gather | solution.py:9
  14.7 135.9 %all-reduce.3.cloned.1.call-start = ((), (), s32[]{:S(2)}) async-start(), calls=%async_computation.1 | async-start | bytes 6291456 | tf_op jit(solution)/shard_map/psum | solution.py:92
  55.6 0.7 copy-start.1
  158.9 8.1 %copy-start.2 = (s32[1024]{0:T(1024)S(1)}, s32[1024]{0:T(1024)}, u32[]{:S(2)}) copy-start(s32[1024]{0:T(1024)} %param.21) | copy-start | bytes 12292
  158.9 162.4 %all-to-all-start = ((bf16[128,8,6144]{2,1,0:T(8,128)(2,1)}), bf16[128,8,6144]{2,1,0:T(8,128)(2,1)}, u32[]{:S(2)}, u32[]{:S(2)}) async-start(bf16[128,8,6144]{2,1,0:T(8,128)(2,1)} %stack.2), calls=%async_computation | async-start | bytes 25165824 | tf_op jit(solution)/shard_map/all_to_all | solution.py:111
Sparse Core Ops, SparseCore 0:
  14.8 26.9 all-gather.3
  55.7 94.8 all-reduce.2
